TPU v7x, 32 devices: a whole 2x2x4 slice. The times are simulated.
32 devices in a mesh: dp: 8 (over z, x), section: 4 (over y, core).
Axes of the slice: x: 2, y: 2, z: 4, core: 2. Of those that a mesh axis runs over, the one named last changes fastest.
Arguments:
- acts: bfloat16 [4, 8, 512, 256], P('section', 'dp'), may hold values from -6 to 6
- out_grad: bfloat16 [8, 512, 256], P('dp'), may hold values from -6 to 6
- weights: bfloat16 [4, 27, 256, 256], P('section'), may hold values from -0.078125 to 0.078125
Outputs:
- level_grads: float32 [4, 8, 512, 256], P('section', 'dp')
- weight_grads: float32 [4, 6912, 256], P('section', 'dp')
All inputs are finite; a program needn't handle non-finite values.
Results may differ from a plain program's by a relative error of at most 0.004.
Values sent between devices are 32-bit elements; how exact they have to be, the bound alone decides.
A program may use at most 128 MiB of HBM per device.

v0:
```python
import functools

import jax
import jax.numpy as jnp
from jax import lax
from jax.experimental import pallas as pl
from jax.experimental.pallas import tpu as pltpu
from jax.sharding import PartitionSpec as P

E = 8
TAPS = 27
PLANE = E * E
GROUP = 4
MESH = pl.DeviceIdType.MESH


def shifted_copies(g_ref, slot, wide):
    chans = g_ref.shape[-1]

    def plane(a, carry):
        rows = pl.ds(pl.multiple_of(a * PLANE, PLANE), PLANE)
        g = g_ref[slot, rows, :].reshape(E, E, chans)
        cell = lax.broadcasted_iota(jnp.int32, (E, E, chans), 1)
        blank = jnp.zeros((1, E, chans), jnp.float32)
        out_rows = pl.ds(pl.multiple_of(a * PLANE + PLANE, PLANE), PLANE)
        for cc in range(3):
            if cc == 0:
                moved = jnp.where(cell == E - 1, 0.0, pltpu.roll(g, E - 1, 1))
            elif cc == 2:
                moved = jnp.where(cell == 0, 0.0, pltpu.roll(g, 1, 1))
            else:
                moved = g
            for bb in range(3):
                if bb == 0:
                    cube = jnp.concatenate([moved[1:], blank], axis=0)
                elif bb == 2:
                    cube = jnp.concatenate([blank, moved[:-1]], axis=0)
                else:
                    cube = moved
                column = (bb * 3 + cc) * chans
                wide[out_rows, column : column + chans] = cube.reshape(PLANE, chans).astype(jnp.bfloat16)
        return carry

    lax.fori_loop(0, E, plane, 0)


def kernel(
    n, levels, rows, span,
    acts, out_grad, weights, level_out, shard_out,
    wcat, hbuf, gbuf, wide, hbf, slope, parts, rbuf,
    w_sem, h_send, h_recv, g_send, g_recv, c_send, c_recv, p_send, p_recv,
):
    groups = n // GROUP
    vox, chans = acts.shape[-2:]
    me = lax.axis_index("dp")
    level = lax.axis_index("section")
    mine = lax.rem(me, GROUP)
    group = me // GROUP
    base = group * GROUP

    barrier = pltpu.get_barrier_semaphore()
    for k in range(1, GROUP):
        pl.semaphore_signal(barrier, inc=1, device_id={"dp": base + lax.rem(mine + k, GROUP)}, device_id_type=MESH)
    for j in range(1, groups):
        pl.semaphore_signal(
            barrier, inc=1, device_id={"dp": lax.rem(group + j, groups) * GROUP + mine}, device_id_type=MESH
        )
    for step in (1, levels - 1):
        pl.semaphore_signal(barrier, inc=1, device_id={"section": lax.rem(level + step, levels)}, device_id_type=MESH)

    def weight_copy(o):
        return pltpu.make_async_copy(
            weights.at[0, o], wcat.at[:, o * chans : (o + 1) * chans], w_sem.at[o]
        )

    for o in range(TAPS):
        weight_copy(o).start()

    @pl.when(level == levels - 1)
    def _():
        gbuf[mine] = out_grad[0].astype(jnp.float32)

    x = acts[0, 0].astype(jnp.float32)
    sig = 1.0 / (1.0 + jnp.exp(-x))
    hidden = (x * sig).astype(jnp.bfloat16).astype(jnp.float32)
    hbuf[mine] = hidden.T
    slope[...] = sig * (1.0 + x * (1.0 - sig))
    edge = jnp.zeros((PLANE, wide.shape[1]), jnp.bfloat16)
    wide[:PLANE, :] = edge
    wide[PLANE + vox :, :] = edge

    pl.semaphore_wait(barrier, GROUP - 1 + groups - 1 + 2)

    def exchange(buf, slot, send, recv, peer):
        return pltpu.make_async_remote_copy(
            src_ref=buf.at[slot], dst_ref=buf.at[slot],
            send_sem=send.at[peer], recv_sem=recv.at[slot],
            device_id={"dp": base + peer}, device_id_type=MESH,
        )

    def peers():
        return [lax.rem(mine + k, GROUP) for k in range(1, GROUP)]

    def chain():
        return pltpu.make_async_remote_copy(
            src_ref=level_out.at[0, 0], dst_ref=gbuf.at[mine],
            send_sem=c_send, recv_sem=c_recv,
            device_id={"section": lax.rem(level + levels - 1, levels)}, device_id_type=MESH,
        )

    for peer in peers():
        exchange(hbuf, mine, h_send, h_recv, peer).start()

    @pl.when(level < levels - 1)
    def _():
        chain().wait_recv()

    for peer in peers():
        exchange(gbuf, mine, g_send, g_recv, peer).start()

    shifted_copies(gbuf, mine, wide)
    for o in range(TAPS):
        weight_copy(o).wait()
    span9 = 9 * chans
    total = None
    for a in range(3):
        term = lax.dot_general(
            wide[(2 - a) * PLANE : (2 - a) * PLANE + vox, :], wcat[:, a * span9 : (a + 1) * span9],
            (((1,), (1,)), ((), ())), preferred_element_type=jnp.float32,
        )
        total = term if total is None else total + term
    level_out[0, 0] = gbuf[mine] + slope[...] * total

    @pl.when(level > 0)
    def _():
        chain().start()

    def owner(j):
        return lax.rem(group + j, groups) * GROUP + mine

    def first_tap(j):
        return owner(j) * rows // chans

    def lead(j):
        return pl.multiple_of(lax.rem(owner(j) * rows, chans), 8)

    def handover(j):
        return pltpu.make_async_remote_copy(
            src_ref=parts.at[j, pl.ds(lead(j), rows)], dst_ref=rbuf.at[j - 1],
            send_sem=p_send.at[j - 1], recv_sem=p_recv.at[j - 1],
            device_id={"dp": owner(j)}, device_id_type=MESH,
        )

    for k in range(GROUP):
        slot = lax.rem(mine + k, GROUP)
        if k > 0:
            exchange(hbuf, slot, h_send, h_recv, slot).wait_recv()
            exchange(gbuf, slot, g_send, g_recv, slot).wait_recv()
            shifted_copies(gbuf, slot, wide)
        hbf[...] = hbuf[slot].astype(jnp.bfloat16)
        for j in list(range(1, groups)) + [0]:
            start = first_tap(j)

            def tap_step(i, carry):
                tap = jnp.minimum(start + i, TAPS - 1)
                plane = pl.ds(pl.multiple_of((2 - tap // 9) * PLANE, PLANE), vox)
                column = pl.ds(pl.multiple_of(lax.rem(tap, 9) * chans, chans), chans)
                place = pl.ds(pl.multiple_of(i * chans, chans), chans)
                term = jnp.dot(hbf[...], wide[plane, column], preferred_element_type=jnp.float32)
                if k == 0:
                    parts[j, place, :] = term
                else:
                    parts[j, place, :] += term
                return carry

            lax.fori_loop(0, span, tap_step, 0)
            if k == GROUP - 1 and j > 0:
                handover(j).start()

    result = parts[0, pl.ds(lead(0), rows), :]
    for j in range(1, groups):
        handover(j).wait_recv()
        result = result + rbuf[j - 1]
    shard_out[0] = result * (1.0 / n)

    for peer in peers():
        exchange(hbuf, mine, h_send, h_recv, peer).wait_send()
        exchange(gbuf, mine, g_send, g_recv, peer).wait_send()
    for j in range(1, groups):
        handover(j).wait_send()

    @pl.when(level > 0)
    def _():
        chain().wait_send()


def body(acts, out_grad, weights):
    n = lax.axis_size("dp")
    levels = lax.axis_size("section")
    vox, chans = acts.shape[2:]
    rows = TAPS * chans // n
    groups = n // GROUP
    span = max((d * rows + rows - 1) // chans - d * rows // chans + 1 for d in range(n))
    sems = pltpu.SemaphoreType.DMA
    return pl.pallas_call(
        functools.partial(kernel, n, levels, rows, span),
        out_shape=(
            jax.ShapeDtypeStruct(acts.shape, jnp.float32),
            jax.ShapeDtypeStruct((1, rows, chans), jnp.float32),
        ),
        in_specs=[
            pl.BlockSpec(memory_space=pltpu.VMEM),
            pl.BlockSpec(memory_space=pltpu.VMEM),
            pl.BlockSpec(memory_space=pl.ANY),
        ],
        out_specs=(pl.BlockSpec(memory_space=pltpu.VMEM), pl.BlockSpec(memory_space=pltpu.VMEM)),
        scratch_shapes=[
            pltpu.VMEM((chans, TAPS * chans), jnp.bfloat16),
            pltpu.VMEM((GROUP, chans, vox), jnp.float32),
            pltpu.VMEM((GROUP, vox, chans), jnp.float32),
            pltpu.VMEM((vox + 2 * PLANE, 9 * chans), jnp.bfloat16),
            pltpu.VMEM((chans, vox), jnp.bfloat16),
            pltpu.VMEM((vox, chans), jnp.float32),
            pltpu.VMEM((groups, span * chans, chans), jnp.float32),
            pltpu.VMEM((max(groups - 1, 1), rows, chans), jnp.float32),
            sems((TAPS,)),
            sems((GROUP,)), sems((GROUP,)), sems((GROUP,)), sems((GROUP,)),
            sems, sems,
            sems((max(groups - 1, 1),)), sems((max(groups - 1, 1),)),
        ],
        compiler_params=pltpu.CompilerParams(
            collective_id=0, has_side_effects=True, vmem_limit_bytes=50 * 1024 * 1024
        ),
        cost_estimate=pl.CostEstimate(flops=4 * 10**9, bytes_accessed=6 * 10**6, transcendentals=vox * chans),
    )(acts, out_grad, weights)


def solution(mesh):
    return jax.shard_map(
        body,
        mesh=mesh,
        in_specs=(
            P("section", "dp", None, None),
            P("dp", None, None),
            P("section", None, None, None),
        ),
        out_specs=(P("section", "dp", None, None), P("section", "dp", None)),
        check_vma=False,
    )
```

profile of v0, /device:TPU:0, one launch (start us, length us, event | category | flops | bytes accessed | tf_op | source)
XLA Modules:
  0.0 102.7 jit_solution(1866382089857164659)
XLA Ops:
  0.6 0.0 copy-start
  0.6 0.9 copy-done
  1.6 0.0 copy-start.1
  1.6 0.9 copy-done.1
  2.5 98.5 %shard_map.50 = (f32[1,1,512,256]{3,2,1,0:T(8,128)S(1)}, f32[1,864,256]{2,1,0:T(8,128)S(1)}) custom-call(bf16[1,1,512,256]{3,2,1,0:T(8,128)(2,1)S(1)} %copy-done, bf16[1,512,256]{2,1,0:T(8,128)(2,1)S(1)} %copy-done.1, bf16[1,27,256,256]{3,2,1,0:T(8,128)(2,1)} %weights.1), custom_call_target="tpu_custom_call" | custom-call | flops 4000000000 | bytes 6000000 | tf_op jit(solution)/shard_map/pallas_call | solution.py:205
  101.0 0.8 copy.7
  101.8 0.9 copy.8
Async XLA Ops:
  0.6 1.0 copy-start
  1.6 0.9 copy-start.1
where the time goes:
time: 103 us
  Pallas kernels  98.5 us (96%)
  local copies, waits for them, and re-layouts  3.6 us (3%)
    pallas_call x1, Pallas kernels, body(): pl.pallas_call(functools.partial(kernel, n, levels, rows, span), out_shap...  98.5 us
    unnamed x6, local copies, waits for them, and re-layouts  3.6 us

commit v1 on v0

v1 whole, which is shorter than its diff:
```python
import functools

import jax
import jax.numpy as jnp
from jax import lax
from jax.experimental import pallas as pl
from jax.experimental.pallas import tpu as pltpu
from jax.sharding import PartitionSpec as P

E = 8
TAPS = 27
PLANE = E * E
GROUP = 4
MESH = pl.DeviceIdType.MESH


def shifted_copies(plane_of, chans, wide):
    def plane(a, carry):
        rows = pl.ds(pl.multiple_of(a * PLANE, PLANE), PLANE)
        g = plane_of(rows).reshape(E, E, chans)
        cell = lax.broadcasted_iota(jnp.int32, (E, E, chans), 1)
        blank = jnp.zeros((1, E, chans), jnp.float32)
        out_rows = pl.ds(pl.multiple_of(a * PLANE + PLANE, PLANE), PLANE)
        for cc in range(3):
            if cc == 0:
                moved = jnp.where(cell == E - 1, 0.0, pltpu.roll(g, E - 1, 1))
            elif cc == 2:
                moved = jnp.where(cell == 0, 0.0, pltpu.roll(g, 1, 1))
            else:
                moved = g
            for bb in range(3):
                if bb == 0:
                    cube = jnp.concatenate([moved[1:], blank], axis=0)
                elif bb == 2:
                    cube = jnp.concatenate([blank, moved[:-1]], axis=0)
                else:
                    cube = moved
                column = (bb * 3 + cc) * chans
                wide[out_rows, column : column + chans] = cube.reshape(PLANE, chans).astype(jnp.bfloat16)
        return carry

    lax.fori_loop(0, E, plane, 0)


def kernel(
    n, levels, rows, span, reach,
    acts, out_grad, weights, level_out, shard_out,
    wcat, hown, hin, gown, gin, wide, narrow, slope, parts, rbuf, done, final,
    w_sem, h_send, h_recv, g_send, g_recv, c_send, c_recv, p_send, p_recv, f_send, f_recv,
):
    groups = n // GROUP
    vox, chans = acts.shape[-2:]
    half = chans // 2
    me = lax.axis_index("dp")
    level = lax.axis_index("section")
    mine = lax.rem(me, GROUP)
    group = me // GROUP
    base = group * GROUP

    barrier = pltpu.get_barrier_semaphore()
    for k in range(1, GROUP):
        pl.semaphore_signal(barrier, inc=1, device_id={"dp": base + lax.rem(mine + k, GROUP)}, device_id_type=MESH)
    for j in range(1, groups):
        pl.semaphore_signal(
            barrier, inc=1, device_id={"dp": lax.rem(group + j, groups) * GROUP + mine}, device_id_type=MESH
        )
    for step in (1, levels - 1):
        pl.semaphore_signal(barrier, inc=1, device_id={"section": lax.rem(level + step, levels)}, device_id_type=MESH)

    def weight_copy(o):
        return pltpu.make_async_copy(
            weights.at[0, o], wcat.at[:, o * chans : (o + 1) * chans], w_sem.at[o]
        )

    for o in range(TAPS):
        weight_copy(o).start()

    @pl.when(level == levels - 1)
    def _():
        gown[...] = out_grad[0].astype(jnp.float32)

    x = acts[0, 0].astype(jnp.float32)
    sig = 1.0 / (1.0 + jnp.exp(-x))
    hidden = (x * sig).astype(jnp.bfloat16).astype(jnp.float32)
    hown[...] = hidden.T

    def row_half(place):
        return pl.ds(pl.multiple_of(lax.rem(place, 2) * half, half), half)

    def column_half(place):
        return pl.ds(pl.multiple_of(place // 2 * half, half), half)

    def send_hidden(peer):
        return pltpu.make_async_remote_copy(
            src_ref=hown.at[row_half(peer)], dst_ref=hin.at[mine],
            send_sem=h_send.at[peer], recv_sem=h_recv.at[mine],
            device_id={"dp": base + peer}, device_id_type=MESH,
        )

    def send_cotangent(peer):
        return pltpu.make_async_remote_copy(
            src_ref=gown.at[:, column_half(peer)], dst_ref=gin.at[mine],
            send_sem=g_send.at[peer], recv_sem=g_recv.at[mine],
            device_id={"dp": base + peer}, device_id_type=MESH,
        )

    def arrived(buf, slot, send, recv):
        pltpu.make_async_remote_copy(
            src_ref=buf.at[slot], dst_ref=buf.at[slot],
            send_sem=send.at[slot], recv_sem=recv.at[slot],
            device_id={"dp": base + slot}, device_id_type=MESH,
        ).wait_recv()

    def chain():
        return pltpu.make_async_remote_copy(
            src_ref=level_out.at[0, 0], dst_ref=gown,
            send_sem=c_send, recv_sem=c_recv,
            device_id={"section": lax.rem(level + levels - 1, levels)}, device_id_type=MESH,
        )

    peers = [lax.rem(mine + k, GROUP) for k in range(1, GROUP)]

    pl.semaphore_wait(barrier, GROUP - 1 + groups - 1 + 2)
    for peer in peers:
        send_hidden(peer).start()

    slope[...] = sig * (1.0 + x * (1.0 - sig))
    for buf in (wide, narrow):
        edge = jnp.zeros((PLANE, buf.shape[1]), jnp.bfloat16)
        buf[:PLANE, :] = edge
        buf[PLANE + vox :, :] = edge

    @pl.when(level < levels - 1)
    def _():
        chain().wait_recv()

    for peer in peers:
        send_cotangent(peer).start()

    shifted_copies(lambda at: gown[at, :], chans, wide)
    for o in range(TAPS):
        weight_copy(o).wait()
    nine = 9 * chans
    total = None
    for a in range(3):
        term = lax.dot_general(
            wide[(2 - a) * PLANE : (2 - a) * PLANE + vox, :], wcat[:, a * nine : (a + 1) * nine],
            (((1,), (1,)), ((), ())), preferred_element_type=jnp.float32,
        )
        total = term if total is None else total + term
    level_out[0, 0] = gown[...] + slope[...] * total

    @pl.when(level > 0)
    def _():
        chain().start()

    def overlaps(place, tap, first, count):
        low = tap * chans + lax.rem(place, 2) * half
        return (low < (first + count) * rows) & (low + half > first * rows)

    def group_tap(g):
        return g * GROUP * rows // chans

    def handover(j, tap):
        to = lax.rem(group + j, groups)
        at = tap - group_tap(to)
        return pltpu.make_async_remote_copy(
            src_ref=parts.at[tap], dst_ref=rbuf.at[j - 1, at],
            send_sem=p_send.at[j - 1, at], recv_sem=p_recv.at[j - 1, at],
            device_id={"dp": to * GROUP + mine}, device_id_type=MESH,
        )

    def needed(j, tap):
        return overlaps(mine, tap, lax.rem(group + j, groups) * GROUP, GROUP)

    leading = group_tap(lax.rem(group + 1, groups)) // 9
    for k in range(GROUP):
        slot = lax.rem(mine + k, GROUP)
        if k == 0:
            left = hown[row_half(mine), :].astype(jnp.bfloat16)
            shifted_copies(lambda at: gown[at, column_half(mine)], half, narrow)
        else:
            arrived(hin, slot, h_send, h_recv)
            left = hin[slot].astype(jnp.bfloat16)
            arrived(gin, slot, g_send, g_recv)
            shifted_copies(lambda at: gin[slot, at, :], half, narrow)
        for step in range(3):
            a = lax.rem(leading + step, 3)
            at = pl.ds(pl.multiple_of((2 - a) * PLANE, PLANE), vox)
            term = jnp.dot(left, narrow[at, :], preferred_element_type=jnp.float32)
            for bc in range(9):
                piece = term[:, bc * half : (bc + 1) * half]
                if k == 0:
                    parts[a * 9 + bc] = piece
                else:
                    parts[a * 9 + bc] += piece
            if k == GROUP - 1:

                def hand_on(bc, carry):
                    tap = a * 9 + bc
                    for j in range(1, groups):

                        @pl.when(needed(j, tap))
                        def _():
                            handover(j, tap).start()

                    return carry

                lax.fori_loop(0, 9, hand_on, 0)

    def owner_tap(place):
        return (base + place) * rows // chans

    def deliver(u, tap, peer):
        at = tap - owner_tap(peer)
        return pltpu.make_async_remote_copy(
            src_ref=done.at[u],
            dst_ref=final.at[pl.ds(pl.multiple_of(at * chans + lax.rem(mine, 2) * half, half), half), column_half(mine)],
            send_sem=f_send.at[peer, at], recv_sem=f_recv.at[mine, at],
            device_id={"dp": base + peer}, device_id_type=MESH,
        )

    def finish(u, carry):
        tap = group_tap(group) + u

        @pl.when(overlaps(mine, tap, base, GROUP))
        def _():
            value = parts[tap]
            for j in range(1, groups):
                pltpu.make_async_remote_copy(
                    src_ref=parts.at[tap], dst_ref=rbuf.at[j - 1, u],
                    send_sem=p_send.at[j - 1, u], recv_sem=p_recv.at[j - 1, u],
                    device_id={"dp": lax.rem(group + j, groups) * GROUP + mine}, device_id_type=MESH,
                ).wait_recv()
                value = value + rbuf[j - 1, u]
            value = value * (1.0 / n)
            done[u] = value
            for peer in peers:

                @pl.when(overlaps(mine, tap, base + peer, 1))
                def _():
                    deliver(u, tap, peer).start()

            @pl.when(overlaps(mine, tap, me, 1))
            def _():
                at = (tap - owner_tap(mine)) * chans + lax.rem(mine, 2) * half
                final[pl.ds(pl.multiple_of(at, half), half), column_half(mine)] = value

        return carry

    lax.fori_loop(0, reach, finish, 0)

    def collect(at, carry):
        tap = owner_tap(mine) + at
        for peer in peers:

            @pl.when(overlaps(peer, tap, me, 1))
            def _():
                pltpu.make_async_remote_copy(
                    src_ref=done.at[0],
                    dst_ref=final.at[
                        pl.ds(pl.multiple_of(at * chans + lax.rem(peer, 2) * half, half), half), column_half(peer)
                    ],
                    send_sem=f_send.at[peer, at], recv_sem=f_recv.at[peer, at],
                    device_id={"dp": base + peer}, device_id_type=MESH,
                ).wait_recv()

        return carry

    lax.fori_loop(0, span, collect, 0)
    shard_out[0] = final[pl.ds(pl.multiple_of(lax.rem(me * rows, chans), 8), rows), :]

    for peer in peers:
        send_hidden(peer).wait_send()
        send_cotangent(peer).wait_send()

    def drain(tap, carry):
        for j in range(1, groups):

            @pl.when(needed(j, tap))
            def _():
                handover(j, tap).wait_send()

        for peer in peers:

            @pl.when(overlaps(mine, tap, base + peer, 1))
            def _():
                deliver(tap - group_tap(group), tap, peer).wait_send()

        return carry

    lax.fori_loop(0, TAPS, drain, 0)

    @pl.when(level > 0)
    def _():
        chain().wait_send()


def body(acts, out_grad, weights):
    n = lax.axis_size("dp")
    levels = lax.axis_size("section")
    vox, chans = acts.shape[2:]
    half = chans // 2
    rows = TAPS * chans // n
    groups = n // GROUP
    others = max(groups - 1, 1)

    def most(width):
        return max((d + width - 1) // chans - d // chans + 1 for d in range(0, TAPS * chans, width))

    span, reach = most(rows), most(rows * GROUP)
    sems = pltpu.SemaphoreType.DMA
    f32, b16 = jnp.float32, jnp.bfloat16
    return pl.pallas_call(
        functools.partial(kernel, n, levels, rows, span, reach),
        out_shape=(
            jax.ShapeDtypeStruct(acts.shape, f32),
            jax.ShapeDtypeStruct((1, rows, chans), f32),
        ),
        in_specs=[
            pl.BlockSpec(memory_space=pltpu.VMEM),
            pl.BlockSpec(memory_space=pltpu.VMEM),
            pl.BlockSpec(memory_space=pl.ANY),
        ],
        out_specs=(pl.BlockSpec(memory_space=pltpu.VMEM), pl.BlockSpec(memory_space=pltpu.VMEM)),
        scratch_shapes=[
            pltpu.VMEM((chans, TAPS * chans), b16),
            pltpu.VMEM((chans, vox), f32),
            pltpu.VMEM((GROUP, half, vox), f32),
            pltpu.VMEM((vox, chans), f32),
            pltpu.VMEM((GROUP, vox, half), f32),
            pltpu.VMEM((vox + 2 * PLANE, 9 * chans), b16),
            pltpu.VMEM((vox + 2 * PLANE, 9 * half), b16),
            pltpu.VMEM((vox, chans), f32),
            pltpu.VMEM((TAPS, half, half), f32),
            pltpu.VMEM((others, reach, half, half), f32),
            pltpu.VMEM((reach, half, half), f32),
            pltpu.VMEM((span * chans, chans), f32),
            sems((TAPS,)),
            sems((GROUP,)), sems((GROUP,)), sems((GROUP,)), sems((GROUP,)),
            sems, sems,
            sems((others, reach)), sems((others, reach)),
            sems((GROUP, span)), sems((GROUP, span)),
        ],
        compiler_params=pltpu.CompilerParams(
            collective_id=0, has_side_effects=True, vmem_limit_bytes=50 * 1024 * 1024
        ),
        cost_estimate=pl.CostEstimate(flops=4 * 10**9, bytes_accessed=6 * 10**6, transcendentals=vox * chans),
    )(acts, out_grad, weights)


def solution(mesh):
    return jax.shard_map(
        body,
        mesh=mesh,
        in_specs=(
            P("section", "dp", None, None),
            P("dp", None, None),
            P("section", None, None, None),
        ),
        out_specs=(P("section", "dp", None, None), P("section", "dp", None)),
        check_vma=False,
    )
```

time: 103 us -> 84.7 us (0.82)
  Pallas kernels: 98.5 us -> 79.7 us
    pallas_call x1, Pallas kernels: 98.5 us -> 79.7 us  [body(): pl.pallas_call(functools.partial(kernel, n, levels, rows, span, reach), o...]
where the time goes in v1:
time: 84.7 us; the launch traced here: 83.9 us
  Pallas kernels  79.7 us (94%)
  local copies, waits for them, and re-layouts  3.6 us (4%)
    pallas_call x1, Pallas kernels, body(): pl.pallas_call(functools.partial(kernel, n, levels, rows, span, reach), o...  79.7 us
    unnamed x6, local copies, waits for them, and re-layouts  3.6 us

profile of v1, /device:TPU:0, one launch (start us, length us, event | category | flops | bytes accessed | tf_op | source)
XLA Modules:
  0.0 83.9 jit_solution(8475698324912835270)
XLA Ops:
  0.6 0.0 copy-start
  0.6 0.9 %copy-done = bf16[1,1,512,256]{3,2,1,0:T(8,128)(2,1)S(1)} copy-done((bf16[1,1,512,256]{3,2,1,0:T(8,128)(2,1)S(1)}, bf16[1,1,512,256]{3,2,1,0:T(8,128)(2,1)}, u32[]{:S(2)}) %copy-start) | copy-done | bytes 262168
  1.6 0.0 copy-start.1
  1.6 0.9 %copy-done.1 = bf16[1,512,256]{2,1,0:T(8,128)(2,1)S(1)} copy-done((bf16[1,512,256]{2,1,0:T(8,128)(2,1)S(1)}, bf16[1,512,256]{2,1,0:T(8,128)(2,1)}, u32[]{:S(2)}) %copy-start.1) | copy-done | bytes 262168
  2.5 79.7 %shard_map.50 = (f32[1,1,512,256]{3,2,1,0:T(8,128)S(1)}, f32[1,864,256]{2,1,0:T(8,128)S(1)}) custom-call(bf16[1,1,512,256]{3,2,1,0:T(8,128)(2,1)S(1)} %copy-done, bf16[1,512,256]{2,1,0:T(8,128)(2,1)S(1)} %copy-done.1, bf16[1,27,256,256]{3,2,1,0:T(8,128)(2,1)} %weights.1), custom_call_target="tpu_custom_call" | custom-call | flops 4000000000 | bytes 6000000 | tf_op jit(solution)/shard_map/pallas_call | solution.py:314
  82.2 0.8 copy.7
  83.0 0.9 %copy.8 = f32[1,864,256]{2,1,0:T(8,128)} copy(f32[1,864,256]{2,1,0:T(8,128)S(1)} %get-tuple-element.5) | data formatting | bytes 1769472
Async XLA Ops:
  0.6 1.0 %copy-start = (bf16[1,1,512,256]{3,2,1,0:T(8,128)(2,1)S(1)}, bf16[1,1,512,256]{3,2,1,0:T(8,128)(2,1)}, u32[]{:S(2)}) copy-start(bf16[1,1,512,256]{3,2,1,0:T(8,128)(2,1)} %acts.1) | copy-start | bytes 786436
  1.6 0.9 %copy-start.1 = (bf16[1,512,256]{2,1,0:T(8,128)(2,1)S(1)}, bf16[1,512,256]{2,1,0:T(8,128)(2,1)}, u32[]{:S(2)}) copy-start(bf16[1,512,256]{2,1,0:T(8,128)(2,1)} %out_grad.1) | copy-start | bytes 786436

commit v2 on v1

--- a/solution.py
+++ b/solution.py
@@ -20,7 +20,6 @@
         g = plane_of(rows).reshape(E, E, chans)
         cell = lax.broadcasted_iota(jnp.int32, (E, E, chans), 1)
         blank = jnp.zeros((1, E, chans), jnp.float32)
-        out_rows = pl.ds(pl.multiple_of(a * PLANE + PLANE, PLANE), PLANE)
         for cc in range(3):
             if cc == 0:
                 moved = jnp.where(cell == E - 1, 0.0, pltpu.roll(g, E - 1, 1))
@@ -36,7 +35,7 @@
                 else:
                     cube = moved
                 column = (bb * 3 + cc) * chans
-                wide[out_rows, column : column + chans] = cube.reshape(PLANE, chans).astype(jnp.bfloat16)
+                wide[rows, column : column + chans] = cube.reshape(PLANE, chans).astype(jnp.bfloat16)
         return carry
 
     lax.fori_loop(0, E, plane, 0)
@@ -69,7 +68,9 @@
 
     def weight_copy(o):
         return pltpu.make_async_copy(
-            weights.at[0, o], wcat.at[:, o * chans : (o + 1) * chans], w_sem.at[o]
+            weights.at[0, o],
+            wcat.at[o // 9 * chans : (o // 9 + 1) * chans, o % 9 * chans : (o % 9 + 1) * chans],
+            w_sem.at[o],
         )
 
     for o in range(TAPS):
@@ -125,10 +126,6 @@
         send_hidden(peer).start()
 
     slope[...] = sig * (1.0 + x * (1.0 - sig))
-    for buf in (wide, narrow):
-        edge = jnp.zeros((PLANE, buf.shape[1]), jnp.bfloat16)
-        buf[:PLANE, :] = edge
-        buf[PLANE + vox :, :] = edge
 
     @pl.when(level < levels - 1)
     def _():
@@ -140,14 +137,15 @@
     shifted_copies(lambda at: gown[at, :], chans, wide)
     for o in range(TAPS):
         weight_copy(o).wait()
-    nine = 9 * chans
-    total = None
-    for a in range(3):
-        term = lax.dot_general(
-            wide[(2 - a) * PLANE : (2 - a) * PLANE + vox, :], wcat[:, a * nine : (a + 1) * nine],
-            (((1,), (1,)), ((), ())), preferred_element_type=jnp.float32,
-        )
-        total = term if total is None else total + term
+    planes = lax.dot_general(
+        wide[...], wcat[...], (((1,), (1,)), ((), ())), preferred_element_type=jnp.float32
+    )
+    edge = jnp.zeros((PLANE, chans), jnp.float32)
+    total = (
+        planes[:, chans : 2 * chans]
+        + jnp.concatenate([planes[PLANE:, :chans], edge], axis=0)
+        + jnp.concatenate([edge, planes[: vox - PLANE, 2 * chans :]], axis=0)
+    )
     level_out[0, 0] = gown[...] + slope[...] * total
 
     @pl.when(level > 0)
@@ -173,40 +171,42 @@
     def needed(j, tap):
         return overlaps(mine, tap, lax.rem(group + j, groups) * GROUP, GROUP)
 
-    leading = group_tap(lax.rem(group + 1, groups)) // 9
+    leading = group_tap(lax.rem(group + 1, groups))
     for k in range(GROUP):
         slot = lax.rem(mine + k, GROUP)
         if k == 0:
-            left = hown[row_half(mine), :].astype(jnp.bfloat16)
+            h = hown[row_half(mine), :]
             shifted_copies(lambda at: gown[at, column_half(mine)], half, narrow)
         else:
             arrived(hin, slot, h_send, h_recv)
-            left = hin[slot].astype(jnp.bfloat16)
+            h = hin[slot]
             arrived(gin, slot, g_send, g_recv)
             shifted_copies(lambda at: gin[slot, at, :], half, narrow)
-        for step in range(3):
-            a = lax.rem(leading + step, 3)
-            at = pl.ds(pl.multiple_of((2 - a) * PLANE, PLANE), vox)
-            term = jnp.dot(left, narrow[at, :], preferred_element_type=jnp.float32)
-            for bc in range(9):
-                piece = term[:, bc * half : (bc + 1) * half]
-                if k == 0:
-                    parts[a * 9 + bc] = piece
-                else:
-                    parts[a * 9 + bc] += piece
-            if k == GROUP - 1:
-
-                def hand_on(bc, carry):
-                    tap = a * 9 + bc
-                    for j in range(1, groups):
-
-                        @pl.when(needed(j, tap))
-                        def _():
-                            handover(j, tap).start()
-
-                    return carry
-
-                lax.fori_loop(0, 9, hand_on, 0)
+        cell = lax.broadcasted_iota(jnp.int32, (half, vox), 1)
+        above = jnp.where(cell < PLANE, 0.0, pltpu.roll(h, PLANE, 1))
+        below = jnp.where(cell >= vox - PLANE, 0.0, pltpu.roll(h, vox - PLANE, 1))
+        left = jnp.concatenate([above, h, below], axis=0).astype(jnp.bfloat16)
+        term = jnp.dot(left, narrow[...], preferred_element_type=jnp.float32)
+        for tap in range(TAPS):
+            a, bc = divmod(tap, 9)
+            piece = term[a * half : (a + 1) * half, bc * half : (bc + 1) * half]
+            if k == 0:
+                parts[tap] = piece
+            else:
+                parts[tap] += piece
+        if k == GROUP - 1:
+
+            def hand_on(i, carry):
+                tap = lax.rem(leading + i, TAPS)
+                for j in range(1, groups):
+
+                    @pl.when(needed(j, tap))
+                    def _():
+                        handover(j, tap).start()
+
+                return carry
+
+            lax.fori_loop(0, TAPS, hand_on, 0)
 
     def owner_tap(place):
         return (base + place) * rows // chans
@@ -324,13 +324,13 @@
         ],
         out_specs=(pl.BlockSpec(memory_space=pltpu.VMEM), pl.BlockSpec(memory_space=pltpu.VMEM)),
         scratch_shapes=[
-            pltpu.VMEM((chans, TAPS * chans), b16),
+            pltpu.VMEM((3 * chans, 9 * chans), b16),
             pltpu.VMEM((chans, vox), f32),
             pltpu.VMEM((GROUP, half, vox), f32),
             pltpu.VMEM((vox, chans), f32),
             pltpu.VMEM((GROUP, vox, half), f32),
-            pltpu.VMEM((vox + 2 * PLANE, 9 * chans), b16),
-            pltpu.VMEM((vox + 2 * PLANE, 9 * half), b16),
+            pltpu.VMEM((vox, 9 * chans), b16),
+            pltpu.VMEM((vox, 9 * half), b16),
             pltpu.VMEM((vox, chans), f32),
             pltpu.VMEM((TAPS, half, half), f32),
             pltpu.VMEM((others, reach, half, half), f32),

time: 84.7 us -> 85.5 us (level)
  no operation moved by 1% of the time
where the time goes in v2:
time: 85.5 us; the launch traced here: 84.8 us
  Pallas kernels  80.5 us (94%)
  local copies, waits for them, and re-layouts  3.6 us (4%)
    pallas_call x1, Pallas kernels, body(): pl.pallas_call(functools.partial(kernel, n, levels, rows, span, reach), o...  80.5 us
    unnamed x6, local copies, waits for them, and re-layouts  3.6 us

profile of v2, /device:TPU:0, one launch (start us, length us, event | category | flops | bytes accessed | tf_op | source)
XLA Modules:
  0.0 84.8 jit_solution(12480259350291007672)
XLA Ops:
  0.6 0.0 copy-start
  0.6 0.9 %copy-done = bf16[1,1,512,256]{3,2,1,0:T(8,128)(2,1)S(1)} copy-done((bf16[1,1,512,256]{3,2,1,0:T(8,128)(2,1)S(1)}, bf16[1,1,512,256]{3,2,1,0:T(8,128)(2,1)}, u32[]{:S(2)}) %copy-start) | copy-done | bytes 262168
  1.6 0.0 copy-start.1
  1.6 0.9 %copy-done.1 = bf16[1,512,256]{2,1,0:T(8,128)(2,1)S(1)} copy-done((bf16[1,512,256]{2,1,0:T(8,128)(2,1)S(1)}, bf16[1,512,256]{2,1,0:T(8,128)(2,1)}, u32[]{:S(2)}) %copy-start.1) | copy-done | bytes 262168
  2.5 80.5 %shard_map.50 = (f32[1,1,512,256]{3,2,1,0:T(8,128)S(1)}, f32[1,864,256]{2,1,0:T(8,128)S(1)}) custom-call(bf16[1,1,512,256]{3,2,1,0:T(8,128)(2,1)S(1)} %copy-done, bf16[1,512,256]{2,1,0:T(8,128)(2,1)S(1)} %copy-done.1, bf16[1,27,256,256]{3,2,1,0:T(8,128)(2,1)} %weights.1), custom_call_target="tpu_custom_call" | custom-call | flops 4000000000 | bytes 6000000 | tf_op jit(solution)/shard_map/pallas_call | solution.py:314
  83.1 0.8 copy.7
  83.9 0.9 %copy.8 = f32[1,864,256]{2,1,0:T(8,128)} copy(f32[1,864,256]{2,1,0:T(8,128)S(1)} %get-tuple-element.5) | data formatting | bytes 1769472
Async XLA Ops:
  0.6 1.0 %copy-start = (bf16[1,1,512,256]{3,2,1,0:T(8,128)(2,1)S(1)}, bf16[1,1,512,256]{3,2,1,0:T(8,128)(2,1)}, u32[]{:S(2)}) copy-start(bf16[1,1,512,256]{3,2,1,0:T(8,128)(2,1)} %acts.1) | copy-start | bytes 786436
  1.6 0.9 %copy-start.1 = (bf16[1,512,256]{2,1,0:T(8,128)(2,1)S(1)}, bf16[1,512,256]{2,1,0:T(8,128)(2,1)}, u32[]{:S(2)}) copy-start(bf16[1,512,256]{2,1,0:T(8,128)(2,1)} %out_grad.1) | copy-start | bytes 786436

commit v3 on v1

--- a/solution.py
+++ b/solution.py
@@ -118,7 +118,7 @@
             device_id={"section": lax.rem(level + levels - 1, levels)}, device_id_type=MESH,
         )
 
-    peers = [lax.rem(mine + k, GROUP) for k in range(1, GROUP)]
+    peers = [mine + 1 - 2 * lax.rem(mine, 2), lax.rem(mine + 2, GROUP), GROUP - 1 - mine]
 
     pl.semaphore_wait(barrier, GROUP - 1 + groups - 1 + 2)
     for peer in peers:
@@ -134,7 +134,7 @@
     def _():
         chain().wait_recv()
 
-    for peer in peers:
+    for peer in peers[:2]:
         send_cotangent(peer).start()
 
     shifted_copies(lambda at: gown[at, :], chans, wide)
@@ -175,7 +175,9 @@
 
     leading = group_tap(lax.rem(group + 1, groups)) // 9
     for k in range(GROUP):
-        slot = lax.rem(mine + k, GROUP)
+        slot = ([mine] + peers)[k]
+        if k == 1:
+            send_cotangent(peers[2]).start()
         if k == 0:
             left = hown[row_half(mine), :].astype(jnp.bfloat16)
             shifted_copies(lambda at: gown[at, column_half(mine)], half, narrow)

time: 84.7 us -> 87.7 us (1.035)
  Pallas kernels: 79.7 us -> 82.7 us
    pallas_call x1, Pallas kernels: 79.7 us -> 82.7 us  [body(): pl.pallas_call(functools.partial(kernel, n, levels, rows, span, reach), o...]
where the time goes in v3:
time: 87.7 us; the launch traced here: 87 us
  Pallas kernels  82.7 us (94%)
  local copies, waits for them, and re-layouts  3.6 us (4%)
    pallas_call x1, Pallas kernels, body(): pl.pallas_call(functools.partial(kernel, n, levels, rows, span, reach), o...  82.7 us
    unnamed x6, local copies, waits for them, and re-layouts  3.6 us

profile of v3, /device:TPU:0, one launch (start us, length us, event | category | flops | bytes accessed | tf_op | source)
XLA Modules:
  0.0 87.0 jit_solution(1656268115111667828)
XLA Ops:
  0.6 0.0 copy-start
  0.6 0.9 %copy-done = bf16[1,1,512,256]{3,2,1,0:T(8,128)(2,1)S(1)} copy-done((bf16[1,1,512,256]{3,2,1,0:T(8,128)(2,1)S(1)}, bf16[1,1,512,256]{3,2,1,0:T(8,128)(2,1)}, u32[]{:S(2)}) %copy-start) | copy-done | bytes 262168
  1.6 0.0 copy-start.1
  1.6 0.9 %copy-done.1 = bf16[1,512,256]{2,1,0:T(8,128)(2,1)S(1)} copy-done((bf16[1,512,256]{2,1,0:T(8,128)(2,1)S(1)}, bf16[1,512,256]{2,1,0:T(8,128)(2,1)}, u32[]{:S(2)}) %copy-start.1) | copy-done | bytes 262168
  2.5 82.7 %shard_map.50 = (f32[1,1,512,256]{3,2,1,0:T(8,128)S(1)}, f32[1,864,256]{2,1,0:T(8,128)S(1)}) custom-call(bf16[1,1,512,256]{3,2,1,0:T(8,128)(2,1)S(1)} %copy-done, bf16[1,512,256]{2,1,0:T(8,128)(2,1)S(1)} %copy-done.1, bf16[1,27,256,256]{3,2,1,0:T(8,128)(2,1)} %weights.1), custom_call_target="tpu_custom_call" | custom-call | flops 4000000000 | bytes 6000000 | tf_op jit(solution)/shard_map/pallas_call | solution.py:316
  85.3 0.8 copy.7
  86.1 0.9 %copy.8 = f32[1,864,256]{2,1,0:T(8,128)} copy(f32[1,864,256]{2,1,0:T(8,128)S(1)} %get-tuple-element.5) | data formatting | bytes 1769472
Async XLA Ops:
  0.6 1.0 %copy-start = (bf16[1,1,512,256]{3,2,1,0:T(8,128)(2,1)S(1)}, bf16[1,1,512,256]{3,2,1,0:T(8,128)(2,1)}, u32[]{:S(2)}) copy-start(bf16[1,1,512,256]{3,2,1,0:T(8,128)(2,1)} %acts.1) | copy-start | bytes 786436
  1.6 0.9 %copy-start.1 = (bf16[1,512,256]{2,1,0:T(8,128)(2,1)S(1)}, bf16[1,512,256]{2,1,0:T(8,128)(2,1)}, u32[]{:S(2)}) copy-start(bf16[1,512,256]{2,1,0:T(8,128)(2,1)} %out_grad.1) | copy-start | bytes 786436
